TPU v7x, 256 devices: a whole 4x4x8 slice. The times are simulated.
256 devices in a mesh: dp: 64 (over z, y, x_hi), tensor: 4 (over x_lo, core).
Axes of the slice: x: 4 (x_hi: 2, x_lo: 2; x = x_hi * 2 + x_lo), y: 4, z: 8, core: 2. Of those that a mesh axis runs over, the one named last changes fastest.
Arguments:
- queries: bfloat16 [2, 4096, 4096], P(None, 'dp', 'tensor'), may hold values from -14 to 14
- cached_key_rows: bfloat16 [4096, 192, 1024], P('dp', None, 'tensor'), may hold values from -6 to 6
- cached_value_rows: bfloat16 [4096, 192, 1024], P('dp', None, 'tensor'), may hold values from -6 to 6
- incoming_keys: bfloat16 [2, 4096, 1024], P(None, 'dp', 'tensor'), may hold values from -6 to 6
- incoming_values: bfloat16 [2, 4096, 1024], P(None, 'dp', 'tensor'), may hold values from -6 to 6
- output_weight: bfloat16 [4096, 4096], P('tensor'), may hold values from -0.125 to 0.125
- adapter_down_weight: bfloat16 [64, 4096, 256], P('dp', 'tensor'), may hold values from -0.09375 to 0.09375
- adapter_up_weight: bfloat16 [64, 256, 4096], P('dp', None, 'tensor'), may hold values from -0.375 to 0.375
- opponent: int32 [4096, 1], P('dp'), may hold values from 0 to 63; in each aligned block of 64 rows (0 to 63, 64 to 127, ...) at most 2 rows name the same one
- cache_length_rows: int32 [4096], P('dp'), may hold values from 1 to 192
Outputs:
- mixed: bfloat16 [2, 4096, 4096], P(None, 'dp', 'tensor')
Inputs may be any that keep to these rules, and one draw needn't show every extreme that they name: In the 64 rows of one index of dp no opponent appears more than 2 times.
All inputs are finite; a program needn't handle non-finite values.
Results may differ from a plain program's by a relative error of at most 0.0061.
Values may be sent and summed in bfloat16 or wider, within the bound.
A program may use at most 192 MiB of HBM per device.

v0:
```python
import math

import jax
import jax.numpy as jnp
from jax import lax
from jax.sharding import PartitionSpec as P

HEAD_SIZE = 128


def attend_cache(query_vector, key_rows, value_rows, step_key_rows, step_value_rows, lengths):
    batch_row_count, width = query_vector.shape
    positions = key_rows.shape[1]
    kv_width = key_rows.shape[2]
    kv_heads = kv_width // HEAD_SIZE
    group_count = width // kv_width
    taken_weight = step_key_rows.shape[0]
    query_head_rows = query_vector.reshape(batch_row_count, kv_heads, group_count, HEAD_SIZE)
    key_head_rows = key_rows.reshape(batch_row_count, positions, kv_heads, HEAD_SIZE)
    value_head_rows = value_rows.reshape(batch_row_count, positions, kv_heads, HEAD_SIZE)
    step_key = step_key_rows.reshape(taken_weight, batch_row_count, kv_heads, HEAD_SIZE)
    step_value = step_value_rows.reshape(taken_weight, batch_row_count, kv_heads, HEAD_SIZE)
    scale = 1.0 / math.sqrt(HEAD_SIZE)
    cache_scores = (
        jnp.einsum(
            "rkgd,rpkd->rkgp", query_head_rows, key_head_rows, preferred_element_type=jnp.float32
        )
        * scale
    )
    live_mask = jnp.arange(positions)[None, :] < lengths[:, None]
    cache_scores = jnp.where(live_mask[:, None, None, :], cache_scores, -1e30)
    fresh_scores = (
        jnp.einsum("rkgd,trkd->rkgt", query_head_rows, step_key, preferred_element_type=jnp.float32)
        * scale
    )
    scores = jnp.concatenate([cache_scores, fresh_scores], axis=3)
    highest = jnp.max(scores, axis=3, keepdims=True)
    powers = jnp.exp(scores - highest)
    probs = (powers / jnp.sum(powers, axis=3, keepdims=True)).astype(jnp.bfloat16)
    result = jnp.einsum(
        "rkgp,rpkd->rkgd",
        probs[..., :positions],
        value_head_rows,
        preferred_element_type=jnp.float32,
    )
    result = result + jnp.einsum(
        "rkgt,trkd->rkgd", probs[..., positions:], step_value, preferred_element_type=jnp.float32
    )
    return result.reshape(batch_row_count, width).astype(jnp.bfloat16)


def project_output_rows(
    attended_output, output_weight, adapter_down_weight, adapter_up_weight, opponent
):
    step_count, batch_row_count, width = attended_output.shape
    local_columns = adapter_up_weight.shape[2]
    peer_count = lax.axis_size("dp")
    flattened = attended_output.reshape(step_count * batch_row_count, width)
    base = lax.psum_scatter(
        lax.dot_general(
            output_weight, flattened, (((0,), (1,)), ((), ())), preferred_element_type=jnp.float32
        ),
        "tensor",
        scatter_dimension=0,
        tiled=True,
    )
    base = base.T.reshape(step_count, batch_row_count, local_columns)
    opponent_ids = opponent[:, 0]
    capacity = max(2, 2 * batch_row_count // peer_count)
    onehot = (opponent_ids[:, None] == jnp.arange(peer_count)[None, :]).astype(jnp.int32)
    rank_within = jnp.sum((jnp.cumsum(onehot, axis=0) - 1) * onehot, axis=1)
    slot_index = opponent_ids * capacity + rank_within
    dispatch = (jnp.arange(peer_count * capacity)[:, None] == slot_index[None, :]).astype(
        jnp.bfloat16
    )
    payload = attended_output.transpose(1, 0, 2).reshape(batch_row_count, step_count * width)
    outgoing = jnp.dot(dispatch, payload, preferred_element_type=jnp.float32).astype(jnp.bfloat16)
    outgoing = outgoing.reshape(peer_count, capacity, step_count * width)
    received = lax.all_to_all(outgoing, "dp", split_axis=0, concat_axis=0, tiled=True)
    sources, slots, unused = received.shape
    partial_sums = jnp.dot(
        received.reshape(sources * slots * step_count, width),
        adapter_down_weight[0],
        preferred_element_type=jnp.float32,
    )
    shrunk_rows = lax.psum(partial_sums, "tensor").astype(jnp.bfloat16)
    lifted_rows = jnp.dot(
        shrunk_rows, adapter_up_weight[0], preferred_element_type=jnp.float32
    ).astype(jnp.bfloat16)
    lifted_rows = lifted_rows.reshape(sources, slots, step_count * local_columns)
    returned = lax.all_to_all(lifted_rows, "dp", split_axis=0, concat_axis=0, tiled=True)
    returned = returned.reshape(peer_count * capacity, step_count * local_columns)
    collected = lax.dot_general(
        dispatch, returned, (((0,), (0,)), ((), ())), preferred_element_type=jnp.float32
    )
    lift = collected.reshape(batch_row_count, step_count, local_columns).transpose(1, 0, 2)
    lift = lift.astype(jnp.bfloat16).astype(jnp.float32)
    return (base + lift).astype(jnp.bfloat16)


def local(
    queries,
    cached_key_rows,
    cached_value_rows,
    incoming_keys,
    incoming_values,
    output_weight,
    adapter_down_weight,
    adapter_up_weight,
    opponent,
    cache_length_rows,
):
    step_count = queries.shape[0]
    attended_outputs = []
    for decode_step_index in range(step_count):
        attended_outputs.append(
            attend_cache(
                queries[decode_step_index],
                cached_key_rows,
                cached_value_rows,
                incoming_keys[: decode_step_index + 1],
                incoming_values[: decode_step_index + 1],
                cache_length_rows,
            )
        )
    pieces_out = []
    for decode_step_index in range(step_count):
        pieces_out.append(
            project_output_rows(
                attended_outputs[decode_step_index][None],
                output_weight,
                adapter_down_weight,
                adapter_up_weight,
                opponent,
            )
        )
    mixed = jnp.concatenate(pieces_out, axis=0)
    return mixed


def solution(mesh):
    in_specs = (
        P(None, "dp", "tensor"),
        P("dp", None, "tensor"),
        P("dp", None, "tensor"),
        P(None, "dp", "tensor"),
        P(None, "dp", "tensor"),
        P("tensor", None),
        P("dp", "tensor", None),
        P("dp", None, "tensor"),
        P("dp", None),
        P("dp"),
    )
    out_specs = P(None, "dp", "tensor")
    return jax.shard_map(local, mesh=mesh, in_specs=in_specs, out_specs=out_specs, check_vma=False)
```

profile of v0, /device:TPU:2, one launch (start us, length us, event | category | flops | bytes accessed | tf_op | source)
XLA Modules:
  0.0 159.2 jit_solution(14349928102831242829)
XLA Ops:
  6.5 0.7 iota_compare_fusion
  7.3 0.9 reshape.118
  8.1 1.0 fusion.52
  9.1 0.1 reshape_squeeze.6
  9.2 0.1 reshape_squeeze.7
  9.3 0.3 fusion.40
  9.6 0.1 copy.54
  9.7 6.1 %fusion.4 = f32[64,2,4,192]{3,2,1,0:T(4,128)S(1)} fusion(bf16[64,2,4,128]{3,2,1,0:T(4,128)(2,1)S(1)} %reshape_squeeze.7, bf16[64,192,256]{2,1,0:T(8,128)(2,1)} %param.11), kind=kOutput, calls=%fused_computation.4 | convolution fusion | flops 25165824 | bytes 6815744 | tf_op jit(solution)/shard_map/rkgd,rpkd->rkgp/dot_general | solution.py:25
  15.8 0.4 copy.52
  16.2 6.1 %fusion.6 = f32[64,2,4,192]{3,2,1,0:T(4,128)S(1)} fusion(bf16[64,2,4,128]{3,2,1,0:T(4,128)(2,1)S(1)} %reshape_squeeze.6, bf16[64,192,256]{2,1,0:T(8,128)(2,1)} %param.11), kind=kOutput, calls=%fused_computation.6 | convolution fusion | flops 25165824 | bytes 6815744 | tf_op jit(solution)/shard_map/rkgd,rpkd->rkgp/dot_general | solution.py:25
  22.3 0.4 copy.44
  22.7 0.8 fusion.50
  23.5 0.4 fusion.35
  23.9 0.4 divide_convert_fusion
  24.3 0.1 slice.34
  24.5 0.3 copy.55
  24.8 0.1 copy.57
  24.9 4.5 %fusion = f32[64,2,4,128]{3,2,1,0:T(4,128)S(1)} fusion(bf16[64,2,4,192]{3,2,1,0:T(4,128)(2,1)S(1)} %copy.55, bf16[64,192,256]{2,1,0:T(8,128)(2,1)} %param.12), kind=kOutput, calls=%fused_computation | convolution fusion | flops 25165824 | bytes 6750208 | tf_op jit(solution)/shard_map/rkgp,rpkd->rkgd/dot_general | solution.py:40
  29.4 0.4 fusion.18
  29.8 0.1 convert_element_type.83
  29.9 5.9 %convolution_bitcast_fusion = f32[4096,64]{0,1:T(8,128)} fusion(bf16[64,1024]{1,0:T(8,128)(2,1)S(1)} %convert_element_type.83, bf16[1024,4096]{1,0:T(8,128)(2,1)} %param.15), kind=kOutput, calls=%fused_computation.12 | convolution fusion | flops 536870912 | bytes 9568256 | tf_op jit(solution)/shard_map/dot_general | solution.py:60
  35.9 0.3 fusion.53
  36.2 0.1 copy.61
  36.3 0.1 broadcast_multiply_fusion
  36.4 0.1 copy.45
  36.5 0.1 copy.47
  36.6 0.4 fusion.36
  37.0 0.4 divide_convert_fusion.1
  37.4 0.1 slice.32
  37.6 0.3 copy.48
  37.9 0.1 copy.50
  38.0 4.5 %fusion.15 = bf16[64,2,4,128]{3,2,1,0:T(4,128)(2,1)S(1)} fusion(bf16[64,2,4,192]{3,2,1,0:T(4,128)(2,1)S(1)} %copy.48, f32[64,2,128]{2,1,0:T(2,128)S(1)} %reshape.125, f32[64,2,4]{2,1,0:T(2,128)S(1)} %copy.50, bf16[64,192,256]{2,1,0:T(8,128)(2,1)} %param.12), kind=kOutput, calls=%fused_computation.20 | convolution fusion | flops 25362432 | bytes 6686720 | tf_op jit(solution)/shard_map/rkgp,rpkd->rkgd/dot_general | solution.py:40
  42.6 0.1 convert_element_type.72
  42.7 0.1 fusion.46
  42.7 0.1 reduce_window_sum.12
  42.8 0.2 select_reduce_fusion
  43.0 0.2 convolution_convert_fusion.3
  43.2 0.8 reshape.114
  44.1 13.8 %all-to-all-start = ((bf16[64,2,1024]{2,1,0:T(2,128)(2,1)}), bf16[64,2,1024]{2,1,0:T(2,128)(2,1)S(1)}, u32[]{:S(2)}, u32[]{:S(2)}) async-start(bf16[64,2,1024]{2,1,0:T(2,128)(2,1)} %reshape.114), calls=%async_computation.1 | async-start | bytes 524288 | tf_op jit(solution)/shard_map/all_to_all | solution.py:79
  57.9 0.2 convolution_convert_fusion.1
  58.1 0.8 reshape.120
  58.9 13.5 %all-to-all-done = bf16[64,2,1024]{2,1,0:T(2,128)(2,1)S(1)} async-done(((bf16[64,2,1024]{2,1,0:T(2,128)(2,1)}), bf16[64,2,1024]{2,1,0:T(2,128)(2,1)S(1)}, u32[]{:S(2)}, u32[]{:S(2)}) %all-to-all-start) | async-done | bytes 262176 | tf_op jit(solution)/shard_map/all_to_all | solution.py:79
  72.5 4.9 %all-to-all-start.2 = ((bf16[64,2,1024]{2,1,0:T(2,128)(2,1)}), bf16[64,2,1024]{2,1,0:T(2,128)(2,1)S(1)}, u32[]{:S(2)}, u32[]{:S(2)}) async-start(bf16[64,2,1024]{2,1,0:T(2,128)(2,1)} %reshape.120), calls=%async_computation.4 | async-start | bytes 524288 | tf_op jit(solution)/shard_map/all_to_all | solution.py:79
  77.3 0.0 reduce-scatter.3.cloned.1.call-start
  77.4 6.0 %convolution_bitcast_fusion.1 = f32[4096,64]{0,1:T(8,128)} fusion(bf16[64,1024]{1,0:T(8,128)(2,1)S(1)} %convert_element_type.72, bf16[1024,4096]{1,0:T(8,128)(2,1)} %param.15), kind=kOutput, calls=%fused_computation.13 | convolution fusion | flops 536870912 | bytes 9568256 | tf_op jit(solution)/shard_map/dot_general | solution.py:60
  83.5 0.1 reshape.115
  83.6 0.2 fusion.33
  83.8 7.5 %all-to-all-done.2 = bf16[64,2,1024]{2,1,0:T(2,128)(2,1)S(1)} async-done(((bf16[64,2,1024]{2,1,0:T(2,128)(2,1)}), bf16[64,2,1024]{2,1,0:T(2,128)(2,1)S(1)}, u32[]{:S(2)}, u32[]{:S(2)}) %all-to-all-start.2) | async-done | bytes 262176 | tf_op jit(solution)/shard_map/all_to_all | solution.py:79
  91.4 0.1 reshape.121
  91.5 0.2 fusion.31
  91.7 16.7 %all-reduce.2 = (bf16[128,256]{1,0:T(8,128)(2,1)S(1)}, bf16[128,256]{1,0:T(8,128)(2,1)S(1)}) all-reduce(f32[128,256]{1,0:T(8,128)S(1)} %fusion.31, f32[128,256]{1,0:T(8,128)S(1)} %fusion.33), channel_id=1, replica_groups=mesh['dp'=64,'tensor'=4] {'tensor'}, use_global_device_ids=true, to_apply=%region_10.11 | all-reduce | flops 65536 | bytes 393216 | tf_op jit(solution)/shard_map/psum | solution.py:86
  108.4 0.2 convolution_convert_fusion
  108.6 0.8 reshape.122
  109.5 4.6 %all-to-all-start.3 = ((bf16[64,2,1024]{2,1,0:T(2,128)(2,1)}), bf16[64,2,1024]{2,1,0:T(2,128)(2,1)S(1)}, u32[]{:S(2)}, u32[]{:S(2)}) async-start(bf16[64,2,1024]{2,1,0:T(2,128)(2,1)} %reshape.122), calls=%async_computation.5 | async-start | bytes 524288 | tf_op jit(solution)/shard_map/all_to_all | solution.py:91
  114.1 0.2 convolution_convert_fusion.2
  114.3 0.8 reshape.116
  115.1 14.2 %all-to-all-done.3 = bf16[64,2,1024]{2,1,0:T(2,128)(2,1)S(1)} async-done(((bf16[64,2,1024]{2,1,0:T(2,128)(2,1)}), bf16[64,2,1024]{2,1,0:T(2,128)(2,1)S(1)}, u32[]{:S(2)}, u32[]{:S(2)}) %all-to-all-start.3) | async-done | bytes 262176 | tf_op jit(solution)/shard_map/all_to_all | solution.py:91
  129.4 5.4 %all-to-all-start.1 = ((bf16[64,2,1024]{2,1,0:T(2,128)(2,1)}), bf16[64,2,1024]{2,1,0:T(2,128)(2,1)S(1)}, u32[]{:S(2)}, u32[]{:S(2)}) async-start(bf16[64,2,1024]{2,1,0:T(2,128)(2,1)} %reshape.116), calls=%async_computation.2 | async-start | bytes 524288 | tf_op jit(solution)/shard_map/all_to_all | solution.py:91
  134.8 0.1 reshape.123
  134.9 14.2 %all-to-all-done.1 = bf16[64,2,1024]{2,1,0:T(2,128)(2,1)S(1)} async-done(((bf16[64,2,1024]{2,1,0:T(2,128)(2,1)}), bf16[64,2,1024]{2,1,0:T(2,128)(2,1)S(1)}, u32[]{:S(2)}, u32[]{:S(2)}) %all-to-all-start.1) | async-done | bytes 262176 | tf_op jit(solution)/shard_map/all_to_all | solution.py:91
  149.1 0.1 reshape.117
  149.2 1.2 fusion.26
  150.4 1.2 fusion.25
  151.6 0.7 pad_maximum_fusion
  (24 shorter events, 0.2 us)
Async XLA Ops:
  6.5 101.9 %copy-start = (bf16[1,256,1024]{2,1,0:T(8,128)(2,1)S(1)}, bf16[1,256,1024]{2,1,0:T(8,128)(2,1)}, u32[]{:S(2)}) copy-start(bf16[1,256,1024]{2,1,0:T(8,128)(2,1)} %param.17) | copy-start | bytes 1572868
  6.5 142.7 %reduce-scatter.5.cloned.1.call-start = ((), (), s32[]{:S(2)}) async-start(), calls=%async_computation.7 | async-start | bytes 1310720 | tf_op jit(solution)/shard_map/reduce_scatter | solution.py:59
  16.2 8.3 %copy-start.2 = (bf16[2,64,256]{2,1,0:T(8,128)(2,1)S(1)}, bf16[2,64,256]{2,1,0:T(8,128)(2,1)}, u32[]{:S(2)}) copy-start(bf16[2,64,256]{2,1,0:T(8,128)(2,1)} %param.14) | copy-start | bytes 196612
  29.9 6.0 %slice-start = ((bf16[2,64,256]{2,1,0:T(8,128)(2,1)}), bf16[1,64,256]{2,1,0:T(8,128)(2,1)S(1)}, s32[]{:S(2)}) async-start(bf16[2,64,256]{2,1,0:T(8,128)(2,1)} %param.13), calls=%async_computation.8 | async-start | bytes 65536 | tf_op jit(solution)/shard_map/slice | solution.py:121
  36.4 6.3 %copy-start.3 = (s32[64,1]{0,1:T(1,128)S(1)}, s32[64,1]{0,1:T(1,128)}, u32[]{:S(2)}) copy-start(s32[64,1]{0,1:T(1,128)} %param.18) | copy-start | bytes 772
  44.1 28.4 %all-to-all-start = ((bf16[64,2,1024]{2,1,0:T(2,128)(2,1)}), bf16[64,2,1024]{2,1,0:T(2,128)(2,1)S(1)}, u32[]{:S(2)}, u32[]{:S(2)}) async-start(bf16[64,2,1024]{2,1,0:T(2,128)(2,1)} %reshape.114), calls=%async_computation.1 | async-start | bytes 524288 | tf_op jit(solution)/shard_map/all_to_all | solution.py:79
  72.5 18.9 %all-to-all-start.2 = ((bf16[64,2,1024]{2,1,0:T(2,128)(2,1)}), bf16[64,2,1024]{2,1,0:T(2,128)(2,1)S(1)}, u32[]{:S(2)}, u32[]{:S(2)}) async-start(bf16[64,2,1024]{2,1,0:T(2,128)(2,1)} %reshape.120), calls=%async_computation.4 | async-start | bytes 524288 | tf_op jit(solution)/shard_map/all_to_all | solution.py:79
  77.3 6.2 %copy-start.1 = (bf16[1,1024,256]{2,1,0:T(8,128)(2,1)S(1)}, bf16[1,1024,256]{2,1,0:T(8,128)(2,1)}, u32[]{:S(2)}) copy-start(bf16[1,1024,256]{2,1,0:T(8,128)(2,1)} %param.16) | copy-start | bytes 1572868
  77.3 73.1 %reduce-scatter.3.cloned.1.call-start = ((), (), s32[]{:S(2)}) async-start(), calls=%async_computation.6 | async-start | bytes 1310720 | tf_op jit(solution)/shard_map/reduce_scatter | solution.py:59
  109.5 19.9 %all-to-all-start.3 = ((bf16[64,2,1024]{2,1,0:T(2,128)(2,1)}), bf16[64,2,1024]{2,1,0:T(2,128)(2,1)S(1)}, u32[]{:S(2)}, u32[]{:S(2)}) async-start(bf16[64,2,1024]{2,1,0:T(2,128)(2,1)} %reshape.122), calls=%async_computation.5 | async-start | bytes 524288 | tf_op jit(solution)/shard_map/all_to_all | solution.py:91
  129.4 19.7 %all-to-all-start.1 = ((bf16[64,2,1024]{2,1,0:T(2,128)(2,1)}), bf16[64,2,1024]{2,1,0:T(2,128)(2,1)S(1)}, u32[]{:S(2)}, u32[]{:S(2)}) async-start(bf16[64,2,1024]{2,1,0:T(2,128)(2,1)} %reshape.116), calls=%async_computation.2 | async-start | bytes 524288 | tf_op jit(solution)/shard_map/all_to_all | solution.py:91
Sparse Core Ops, SparseCore 0:
  36.0 24.6 reduce-scatter.4
  83.6 26.2 reduce-scatter.2
where the time goes:
time: 160 us; the launch traced here: 159 us
  waiting for transfers between devices  49.6 us (31%)
  matrix products  37.9 us (24%)
  starting transfers between devices  28.8 us (18%)
  blocking collectives  16.7 us (10%)
  between operations  13.8 us (9%)
  local copies, waits for them, and re-layouts  8.17 us (5%)
  other arithmetic  4.27 us (3%)
    all_to_all x2, waiting for transfers between devices, project_output_rows(): lax.all_to_all(lifted_rows, 'dp', split_axis=0, concat_axis=0, tiled=True)  28.4 us
    all_to_all x2, waiting for transfers between devices, project_output_rows(): lax.all_to_all(outgoing, 'dp', split_axis=0, concat_axis=0, tiled=True)  21.1 us
    all_to_all x2, starting transfers between devices, project_output_rows(): lax.all_to_all(outgoing, 'dp', split_axis=0, concat_axis=0, tiled=True)  18.7 us
    psum x1, blocking collectives, project_output_rows(): shrunk_rows = lax.psum(partial_sums, 'tensor').astype(jnp.bfloat16)  16.7 us
    dot_general x2, matrix products, attend_cache(): jnp.einsum('rkgd,rpkd->rkgp', query_head_rows, key_head_rows, preferred_e...  12.2 us
    dot_general x2, matrix products, project_output_rows(): lax.dot_general(output_weight, flattened, (((0,), (1,)), ((), ())), prefe...  12 us
    all_to_all x2, starting transfers between devices, project_output_rows(): lax.all_to_all(lifted_rows, 'dp', split_axis=0, concat_axis=0, tiled=True)  10.1 us
    dot_general x2, matrix products, attend_cache(): jnp.einsum('rkgp,rpkd->rkgd', probs[..., :positions], value_head_rows, pr...  9.03 us
  transfers between devices with their start and end apart: 6, of which 4 were waited for; matrix products, arithmetic and copies ran while one was open for 12% of the time, Pallas kernels for 0%

commit v1 on v0

v1 whole, which is shorter than its diff:
```python
import math

import jax
import jax.numpy as jnp
from jax import lax
from jax.experimental import pallas as pl
from jax.experimental.pallas import tpu as pltpu
from jax.sharding import PartitionSpec as P

ROWS = 64
CACHE = 192
EXTENDED = 208
GROUP = 16
HEAD = 128
SCALE = 1.0 / math.sqrt(HEAD)
MESH = pl.DeviceIdType.MESH
CONTRACT_LAST = (((1,), (1,)), ((), ()))


def kernel(
    q_hbm, k_hbm, v_hbm, nk_hbm, nv_hbm, wo_hbm, wd_hbm, wu_hbm, len_ref, place_row, place_col,
    out_ref,
    qv, nkv, nvv, kb, vb, fresh, qs, att, attp, outward, homeward, wo, wd, wu,
    send, recv, recvf, part, x1r, x2s, x2r, shrunk, liftf, rsend, rrecv,
    attb, bsend, brecv, keep, csend, crecv,
    small_sem, kv_sem, w_sem, d_send, d_recv, r_send, r_recv, t_send, t_recv,
):
    dp = lax.axis_index("dp")
    t = lax.axis_index("tensor")
    z, y, xh = dp // 8, lax.rem(dp // 2, 4), lax.rem(dp, 2)
    core = lax.rem(t, 2)
    near = t + 1 - 2 * core
    far = lax.rem(t + 2, 4)
    near_far = lax.rem(near + 2, 4)

    def peer(j):
        k = j + (j + 57) // 64
        a, b = lax.rem(k, 8), k // 8
        dz = lax.rem(12 + ((a + 1) // 2) * (1 - 2 * lax.rem(a, 2)), 8)
        return lax.rem(z + dz, 8) * 8 + lax.rem(y + b // 2, 4) * 2 + lax.rem(xh + lax.rem(b, 2), 2)

    small = [
        pltpu.make_async_copy(a, b, small_sem.at[i])
        for i, (a, b) in enumerate(((q_hbm, qv), (nk_hbm, nkv), (nv_hbm, nvv)))
    ]
    for c in small:
        c.start()

    def kv_copies(g):
        rows = pl.ds(g * GROUP, GROUP)
        return (
            pltpu.make_async_copy(k_hbm.at[rows], kb.at[rows, pl.ds(0, CACHE)], kv_sem.at[0, g]),
            pltpu.make_async_copy(v_hbm.at[rows], vb.at[rows, pl.ds(0, CACHE)], kv_sem.at[1, g]),
        )

    for g in range(ROWS // GROUP):
        for c in kv_copies(g):
            c.start()
    weights = [
        pltpu.make_async_copy(
            wo_hbm.at[:, pl.ds(pl.multiple_of(block * 1024, 1024), 1024)], wo.at[i], w_sem.at[i]
        )
        for i, block in enumerate((near, near_far, far, t))
    ]
    weights.append(pltpu.make_async_copy(wd_hbm.at[0], wd, w_sem.at[4]))
    weights.append(pltpu.make_async_copy(wu_hbm.at[0], wu, w_sem.at[5]))
    for c in weights:
        c.start()

    barrier = pltpu.get_barrier_semaphore()

    def greet(j, carry):
        pl.semaphore_signal(barrier, inc=1, device_id=(peer(j), t), device_id_type=MESH)
        return carry

    lax.fori_loop(0, 63, greet, 0)
    for other in (near, far, near_far):
        pl.semaphore_signal(barrier, inc=1, device_id=(dp, other), device_id_type=MESH)

    for c in small:
        c.wait()
    for h in range(2):
        for s in range(2):
            for g in range(4):
                col = (h * 4 + g) * HEAD
                qs[h, pl.ds(s * 4 + g, ROWS, stride=8), :] = qv[s, :, col : col + HEAD].astype(jnp.float32)
    fresh[...] = jnp.zeros_like(fresh)
    for src, dst in ((nkv, kb), (nvv, vb)):
        for s in range(2):
            for h in range(2):
                fresh[h, pl.ds(s, ROWS, stride=16), :] = src[s, :, h * HEAD : (h + 1) * HEAD].astype(jnp.float32)
        for h in range(2):
            dst[:, CACHE:EXTENDED, h * HEAD : (h + 1) * HEAD] = (
                fresh[h].reshape(ROWS, 16, HEAD).astype(jnp.bfloat16)
            )

    def map_out(i, carry):
        rows = pl.ds(pl.multiple_of(i * 64, 64), 64)
        at = lax.broadcasted_iota(jnp.int32, (64, ROWS * 8), 0) + i * 64
        outward[rows, :] = jnp.where(at == place_row[...], 1.0, 0.0).astype(jnp.bfloat16)
        return carry

    lax.fori_loop(0, 16, map_out, 0)

    def map_home(i, carry):
        rows = pl.ds(pl.multiple_of(i * 32, 32), 32)
        at = lax.broadcasted_iota(jnp.int32, (32, ROWS * 16), 1)
        homeward[rows, :] = jnp.where(at == place_col[rows, :], 1.0, 0.0).astype(jnp.bfloat16)
        return carry

    lax.fori_loop(0, 16, map_home, 0)

    lane = lax.broadcasted_iota(jnp.int32, (8, EXTENDED), 1)
    sub = lax.broadcasted_iota(jnp.int32, (8, EXTENDED), 0)
    new_ok = (lane == CACHE) | ((lane == CACHE + 1) & (sub >= 4))
    zero = jnp.zeros((8, HEAD), jnp.float32)

    def probs(scores, r):
        ok = (lane < len_ref[r]) | new_ok
        scores = jnp.where(ok, scores * SCALE, -1e30)
        power = jnp.exp(scores - jnp.max(scores, axis=1, keepdims=True))
        return power / jnp.sum(power, axis=1, keepdims=True)

    def attend(g, carry):
        for c in kv_copies(g):
            c.wait()
        rows = [g * GROUP + j for j in range(GROUP)]
        at = [pl.ds(pl.multiple_of(r * 8, 8), 8) for r in rows]
        scores = []
        for r, a in zip(rows, at):
            q = jnp.concatenate(
                [jnp.concatenate([qs[0, a, :], zero], 1), jnp.concatenate([zero, qs[1, a, :]], 1)], 0
            ).astype(jnp.bfloat16)
            scores.append(lax.dot_general(q, kb[r], CONTRACT_LAST, preferred_element_type=jnp.float32))
        ps = [
            jnp.concatenate([probs(s[:8], r), probs(s[8:], r)], 0).astype(jnp.bfloat16)
            for s, r in zip(scores, rows)
        ]
        both = []
        for p, r, a in zip(ps, rows, at):
            o = jnp.dot(p, vb[r], preferred_element_type=jnp.float32)
            att[0, a, :] = o[:8, :HEAD]
            att[1, a, :] = o[8:, HEAD:]
            both.append(jnp.concatenate([o[:8, :HEAD], o[8:, HEAD:]], 1))
        for i in range(GROUP // 2):
            pair = pl.ds(pl.multiple_of(g * GROUP * 8 + i * 16, 16), 16)
            attp[pair, :] = jnp.concatenate(both[2 * i : 2 * i + 2], 0).astype(jnp.bfloat16)
        return carry

    lax.fori_loop(0, ROWS // GROUP, attend, 0)

    pl.semaphore_wait(barrier, 66)

    def fill(i, carry):
        rows = pl.ds(pl.multiple_of(i * 256, 256), 256)
        filled = jnp.dot(outward[rows, :], attp[...], preferred_element_type=jnp.float32)
        send[pl.ds(pl.multiple_of(i * 16, 16), 16)] = filled.astype(jnp.bfloat16).reshape(16, 16, 256)
        return carry

    lax.fori_loop(0, 4, fill, 0)

    def dispatch(i, carry):
        for j in range(7):
            d = peer(i * 7 + j)
            pltpu.make_async_remote_copy(
                src_ref=send.at[d], dst_ref=recv.at[dp], send_sem=d_send, recv_sem=d_recv,
                device_id=(d, t), device_id_type=MESH,
            ).start()
        return carry

    lax.fori_loop(0, 9, dispatch, 0)
    recv[dp] = send[dp]

    for h in range(2):
        for s in range(2):
            for g in range(4):
                col = (h * 4 + g) * HEAD
                attb[s * ROWS : (s + 1) * ROWS, col : col + HEAD] = att[
                    h, pl.ds(s * 4 + g, ROWS, stride=8), :
                ].astype(jnp.bfloat16)

    def base_block(i, store):
        weights[i].wait()

        def tile(n, carry):
            cols = pl.ds(pl.multiple_of(n * 256, 256), 256)
            store(cols, jnp.dot(attb[...], wo[i, :, cols], preferred_element_type=jnp.float32))
            return carry

        lax.fori_loop(0, 4, tile, 0)

    def remote(i, src, dst, other):
        return pltpu.make_async_remote_copy(
            src_ref=src, dst_ref=dst, send_sem=t_send.at[i], recv_sem=t_recv.at[i],
            device_id=(dp, other), device_id_type=MESH,
        )

    base_near = []
    for i in range(2):

        def to_send(cols, value, i=i):
            bsend[i, :, cols] = value.astype(jnp.bfloat16)

        base_block(i, to_send)
        c = remote(i, bsend.at[i], brecv.at[i], near)
        c.start()
        base_near.append(c)
    for i in range(2):

        def to_keep(cols, value, i=i):
            keep[i, :, cols] = value

        base_block(2 + i, to_keep)
    base_near[1].wait()
    csend[...] = (keep[0] + brecv[1].astype(jnp.float32)).astype(jnp.bfloat16)
    base_far = remote(2, csend, crecv, far)
    base_far.start()

    weights[4].wait()
    weights[5].wait()
    pltpu.make_async_copy(recv.at[pl.ds(0, 63)], recv.at[pl.ds(0, 63)], d_recv).wait()
    for h in range(2):
        recvf[h] = recv[:, :, h * HEAD : (h + 1) * HEAD].reshape(16 * ROWS, HEAD).astype(jnp.float32)
    received = jnp.concatenate(
        [recvf[h, pl.ds(g, 4 * ROWS, stride=4), :].astype(jnp.bfloat16) for h in range(2) for g in range(4)], 1
    )
    part[...] = jnp.dot(received, wd[...], preferred_element_type=jnp.float32)
    mine = pl.ds(pl.multiple_of(core * 128, 128), 128)
    theirs = pl.ds(pl.multiple_of((1 - core) * 128, 128), 128)
    x1 = remote(3, part.at[theirs], x1r, near)
    x1.start()
    x1.wait()
    pair_sum = part[mine, :] + x1r[...]
    x2s[...] = pair_sum.astype(jnp.bfloat16)
    x2 = remote(4, x2s, x2r, far)
    x2.start()
    x2.wait()
    shrunk[mine, :] = (part[mine, :] + x1r[...] + x2r[...].astype(jnp.float32)).astype(jnp.bfloat16)
    x3 = remote(5, shrunk.at[mine], shrunk.at[mine], near)
    x3.start()
    x3.wait()

    for c in range(4):
        lifted = jnp.dot(shrunk[...], wu[:, c * 256 : (c + 1) * 256], preferred_element_type=jnp.float32)
        for h in range(2):
            liftf[h, pl.ds(c, 4 * ROWS, stride=4), :] = lifted[:, h * HEAD : (h + 1) * HEAD]
    for h in range(2):
        rsend[:, :, h * HEAD : (h + 1) * HEAD] = liftf[h].reshape(ROWS, 16, HEAD).astype(jnp.bfloat16)
    rrecv[dp] = rsend[dp]

    def give_back(i, carry):
        for j in range(7):
            d = peer(i * 7 + j)
            pltpu.make_async_remote_copy(
                src_ref=rsend.at[d], dst_ref=rrecv.at[dp], send_sem=r_send, recv_sem=r_recv,
                device_id=(d, t), device_id_type=MESH,
            ).start()
        return carry

    lax.fori_loop(0, 9, give_back, 0)

    base_near[0].wait()
    base_far.wait()
    keep[1] = keep[1] + brecv[0].astype(jnp.float32) + crecv[...].astype(jnp.float32)
    pltpu.make_async_copy(rrecv.at[pl.ds(0, 63)], rrecv.at[pl.ds(0, 63)], r_recv).wait()

    for c in range(4):
        cols = slice(c * 256, (c + 1) * 256)
        lifts = jnp.dot(
            homeward[c * 128 : (c + 1) * 128, :], rrecv[...].reshape(ROWS * 16, 256), preferred_element_type=jnp.float32
        )
        for s in range(2):
            rows = slice(s * ROWS, (s + 1) * ROWS)
            out_ref[s, :, cols] = (keep[1, rows, cols] + lifts[rows]).astype(jnp.bfloat16)
    pltpu.make_async_copy(send.at[pl.ds(0, 63)], send.at[pl.ds(0, 63)], d_send).wait()
    pltpu.make_async_copy(rsend.at[pl.ds(0, 63)], rsend.at[pl.ds(0, 63)], r_send).wait()


def local(
    queries,
    cached_key_rows,
    cached_value_rows,
    incoming_keys,
    incoming_values,
    output_weight,
    adapter_down_weight,
    adapter_up_weight,
    opponent,
    cache_length_rows,
):
    ids = opponent[:, 0]
    place = jnp.arange(ROWS, dtype=jnp.int32)
    earlier = (ids[:, None] == ids[None, :]) & (place[None, :] < place[:, None])
    slot_of_row = 2 * ids + jnp.sum(earlier.astype(jnp.int32), axis=1)
    eight = jnp.arange(8, dtype=jnp.int32)
    place_row = (slot_of_row[:, None] * 8 + eight[None, :]).reshape(1, ROWS * 8)
    quarter, step = jnp.arange(4, dtype=jnp.int32), jnp.arange(2, dtype=jnp.int32)
    place_col = (
        slot_of_row[None, None, :] * 8 + step[None, :, None] * 4 + quarter[:, None, None]
    ).reshape(ROWS * 8, 1)
    bf16, f32 = jnp.bfloat16, jnp.float32
    vmem, dma = pltpu.VMEM, pltpu.SemaphoreType.DMA
    hbm = pl.BlockSpec(memory_space=pl.ANY)
    smem = pl.BlockSpec(memory_space=pltpu.SMEM)
    return pl.pallas_call(
        kernel,
        out_shape=jax.ShapeDtypeStruct((2, ROWS, 1024), bf16),
        in_specs=[hbm] * 8 + [smem] + [pl.BlockSpec(memory_space=pltpu.VMEM)] * 2,
        out_specs=pl.BlockSpec(memory_space=pltpu.VMEM),
        scratch_shapes=[
            vmem((2, ROWS, 1024), bf16),
            vmem((2, ROWS, 256), bf16),
            vmem((2, ROWS, 256), bf16),
            vmem((ROWS, EXTENDED, 256), bf16),
            vmem((ROWS, EXTENDED, 256), bf16),
            vmem((2, ROWS * 16, HEAD), f32),
            vmem((2, ROWS * 8, HEAD), f32),
            vmem((2, ROWS * 8, HEAD), f32),
            vmem((ROWS * 8, 256), bf16),
            vmem((ROWS * 16, ROWS * 8), bf16),
            vmem((ROWS * 8, ROWS * 16), bf16),
            vmem((4, 1024, 1024), bf16),
            vmem((1024, 256), bf16),
            vmem((256, 1024), bf16),
            vmem((ROWS, 16, 256), bf16),
            vmem((ROWS, 16, 256), bf16),
            vmem((2, ROWS * 16, HEAD), f32),
            vmem((256, 256), f32),
            vmem((128, 256), f32),
            vmem((128, 256), bf16),
            vmem((128, 256), bf16),
            vmem((256, 256), bf16),
            vmem((2, ROWS * 16, HEAD), f32),
            vmem((ROWS, 16, 256), bf16),
            vmem((ROWS, 16, 256), bf16),
            vmem((2 * ROWS, 1024), bf16),
            vmem((2, 2 * ROWS, 1024), bf16),
            vmem((2, 2 * ROWS, 1024), bf16),
            vmem((2, 2 * ROWS, 1024), f32),
            vmem((2 * ROWS, 1024), bf16),
            vmem((2 * ROWS, 1024), bf16),
            dma((3,)),
            dma((2, 4)),
            dma((6,)),
            dma,
            dma,
            dma,
            dma,
            dma((6,)),
            dma((6,)),
        ],
        compiler_params=pltpu.CompilerParams(
            collective_id=0, has_side_effects=True, vmem_limit_bytes=56 << 20
        ),
        cost_estimate=pl.CostEstimate(flops=1500000000, bytes_accessed=24000000, transcendentals=300000),
    )(
        queries,
        cached_key_rows,
        cached_value_rows,
        incoming_keys,
        incoming_values,
        output_weight,
        adapter_down_weight,
        adapter_up_weight,
        cache_length_rows,
        place_row,
        place_col,
    )


def solution(mesh):
    in_specs = (
        P(None, "dp", "tensor"),
        P("dp", None, "tensor"),
        P("dp", None, "tensor"),
        P(None, "dp", "tensor"),
        P(None, "dp", "tensor"),
        P("tensor", None),
        P("dp", "tensor", None),
        P("dp", None, "tensor"),
        P("dp", None),
        P("dp"),
    )
    out_specs = P(None, "dp", "tensor")
    return jax.shard_map(local, mesh=mesh, in_specs=in_specs, out_specs=out_specs, check_vma=False)
```

time: 160 us -> 66.5 us (0.42)
  the two profiles are of different devices: /device:TPU:2 before, /device:TPU:1 now
where the time goes in v1:
time: 66.5 us; the launch traced here: 66.4 us
  Pallas kernels  60.7 us (91%)
  local copies, waits for them, and re-layouts  3.25 us (5%)
  other arithmetic  2.39 us (4%)
    pallas_call x1, Pallas kernels, local(): pl.pallas_call(kernel, out_shape=jax.ShapeDtypeStruct((2, ROWS, 1024), bf...  60.7 us
    unnamed x1, local copies, waits for them, and re-layouts  1.67 us

profile of v1, /device:TPU:1, one launch (start us, length us, event | category | flops | bytes accessed | tf_op | source)
XLA Modules:
  0.0 66.4 jit_solution(9147138737092343940)
XLA Ops:
  0.0 0.9 %convert_reduce_fusion = s32[64]{0:T(128)S(1)} fusion(s32[64]{0:T(128)} %bitcast.10), kind=kLoop, calls=%fused_computation.1 | loop fusion | flops 20416 | bytes 512 | tf_op jit(solution)/shard_map/reduce_sum | solution.py:294
  0.9 0.7 %add_multiply_fusion = s32[64]{0:T(128)S(1)} fusion(s32[64]{0:T(128)S(1)} %convert_reduce_fusion, s32[64,1]{0,1:T(1,128)} %param.18), kind=kLoop, calls=%fused_computation.10 | loop fusion | flops 192 | bytes 768 | tf_op jit(solution)/shard_map/mul | solution.py:299
  1.6 0.7 fusion.2
  2.2 0.1 broadcast_add_fusion
  2.3 0.1 iota_add_fusion
  2.4 0.7 %add.81.place_row = s32[1,512]{1,0:T(1,128)} reshape(s32[64,8]{1,0:T(8,128)S(1)} %iota_add_fusion) | data formatting | bytes 4096 | tf_op jit(solution)/shard_map/add | solution.py:296
  3.1 0.9 %add.90.place_col = s32[512,1]{1,0:T(8,128)} reshape(s32[4,2,64]{2,1,0:T(2,128)S(1)} %iota_add_fusion.1) | data formatting | bytes 4096 | tf_op jit(solution)/shard_map/add | solution.py:299
  4.0 60.7 %shard_map.100 = bf16[2,64,1024]{2,1,0:T(8,128)(2,1)} custom-call(bf16[2,64,1024]{2,1,0:T(8,128)(2,1)} %q_hbm.1, bf16[64,192,256]{2,1,0:T(8,128)(2,1)} %k_hbm.1, bf16[64,192,256]{2,1,0:T(8,128)(2,1)} %v_hbm.1, bf16[2,64,256]{2,1,0:T(8,128)(2,1)} %nk_hbm.1, bf16[2,64,256]{2,1,0:T(8,128)(2,1)} %nv_hbm.1, bf16[1024,4096]{1,0:T(8,128)(2,1)} %wo_hbm.1, ...), custom_call_target="tpu_custom_call" | custom-call | flops 1500000000 | bytes 24000000 | tf_op jit(solution)/shard_map/pallas_call | solution.py:305
  64.7 1.7 %copy.14 = bf16[2,64,1024]{2,1,0:T(8,128)(2,1)} copy(bf16[2,64,1024]{2,1,0:T(8,128)(2,1)} %shard_map.100) | data formatting | bytes 524288
  (2 shorter events, 0.0 us)

commit v2 on v1

--- a/solution.py
+++ b/solution.py
@@ -18,10 +18,10 @@
 
 
 def kernel(
-    q_hbm, k_hbm, v_hbm, nk_hbm, nv_hbm, wo_hbm, wd_hbm, wu_hbm, len_ref, place_row, place_col,
+    q_hbm, k_hbm, v_hbm, nk_hbm, nv_hbm, wo_hbm, wd_hbm, wu_hbm, len_ref, opp_ref,
     out_ref,
-    qv, nkv, nvv, kb, vb, fresh, qs, att, attp, outward, homeward, wo, wd, wu,
-    send, recv, recvf, part, x1r, x2s, x2r, shrunk, liftf, rsend, rrecv,
+    qv, nkv, nvv, kb, vb, fresh, qs, att, attp, place_row, place_col, outward, homeward, wo, wd, wu,
+    send, recv, recvf, part, x1r, shrunk, liftf, rsend, rrecv,
     attb, bsend, brecv, keep, csend, crecv,
     small_sem, kv_sem, w_sem, d_send, d_recv, r_send, r_recv, t_send, t_recv,
 ):
@@ -33,11 +33,27 @@
     far = lax.rem(t + 2, 4)
     near_far = lax.rem(near + 2, 4)
 
-    def peer(j):
-        k = j + (j + 57) // 64
-        a, b = lax.rem(k, 8), k // 8
-        dz = lax.rem(12 + ((a + 1) // 2) * (1 - 2 * lax.rem(a, 2)), 8)
-        return lax.rem(z + dz, 8) * 8 + lax.rem(y + b // 2, 4) * 2 + lax.rem(xh + lax.rem(b, 2), 2)
+    order = (4, 3, 5, 2, 6, 1, 7, 0)
+    ahead = [lax.rem(z + dz, 8) * 8 for dz in order]
+    behind = [lax.rem(z + 8 - dz, 8) * 8 for dz in order]
+
+    def across(b, sign):
+        c = b // 2
+        dy = lax.rem(2 * c, 4) + c // 2
+        return lax.rem(y + 4 + sign * dy, 4) * 2 + lax.rem(xh + lax.rem(b, 2), 2)
+
+    def each(first, last, planes, sign, step):
+        if first == 0:
+            for a in range(7):
+                step(a, planes[a] + across(0, sign))
+
+        def body(b, carry):
+            plane = across(b, sign)
+            for a in range(8):
+                step(b * 8 + a, planes[a] + plane)
+            return carry
+
+        lax.fori_loop(max(first, 1), last, body, 0)
 
     small = [
         pltpu.make_async_copy(a, b, small_sem.at[i])
@@ -64,16 +80,12 @@
     ]
     weights.append(pltpu.make_async_copy(wd_hbm.at[0], wd, w_sem.at[4]))
     weights.append(pltpu.make_async_copy(wu_hbm.at[0], wu, w_sem.at[5]))
-    for c in weights:
-        c.start()
-
     barrier = pltpu.get_barrier_semaphore()
 
-    def greet(j, carry):
-        pl.semaphore_signal(barrier, inc=1, device_id=(peer(j), t), device_id_type=MESH)
-        return carry
-
-    lax.fori_loop(0, 63, greet, 0)
+    def greet(k, d):
+        pl.semaphore_signal(barrier, inc=1, device_id=(d, t), device_id_type=MESH)
+
+    each(0, 8, ahead, 1, greet)
     for other in (near, far, near_far):
         pl.semaphore_signal(barrier, inc=1, device_id=(dp, other), device_id_type=MESH)
 
@@ -94,21 +106,20 @@
                 fresh[h].reshape(ROWS, 16, HEAD).astype(jnp.bfloat16)
             )
 
-    def map_out(i, carry):
-        rows = pl.ds(pl.multiple_of(i * 64, 64), 64)
-        at = lax.broadcasted_iota(jnp.int32, (64, ROWS * 8), 0) + i * 64
-        outward[rows, :] = jnp.where(at == place_row[...], 1.0, 0.0).astype(jnp.bfloat16)
-        return carry
-
-    lax.fori_loop(0, 16, map_out, 0)
-
-    def map_home(i, carry):
-        rows = pl.ds(pl.multiple_of(i * 32, 32), 32)
-        at = lax.broadcasted_iota(jnp.int32, (32, ROWS * 16), 1)
-        homeward[rows, :] = jnp.where(at == place_col[rows, :], 1.0, 0.0).astype(jnp.bfloat16)
-        return carry
-
-    lax.fori_loop(0, 16, map_home, 0)
+    ids = opp_ref[...]
+    down = lax.broadcasted_iota(jnp.int32, (ROWS, ROWS), 0)
+    along = lax.broadcasted_iota(jnp.int32, (ROWS, ROWS), 1)
+    named = jnp.where(down == ids, 1.0, 0.0)
+    before = jnp.where(down < along, 1.0, 0.0).astype(jnp.bfloat16)
+    earlier = jnp.dot(named.astype(jnp.bfloat16), before, preferred_element_type=jnp.float32)
+    rank = jnp.sum(named * earlier, axis=0, keepdims=True).astype(jnp.int32)
+    slot = jnp.sum(jnp.where(down == along, 2 * ids + rank, 0), axis=1, keepdims=True)
+    place_col[...] = jnp.broadcast_to(slot * 8, (ROWS, HEAD))
+    lanes = lax.broadcasted_iota(jnp.int32, (ROWS, ROWS * 8), 1)
+    rows_of = lax.broadcasted_iota(jnp.int32, (ROWS, ROWS * 8), 0)
+    place_row[...] = jnp.sum(
+        jnp.where((lanes >> 3) == rows_of, slot * 8 + (lanes & 7), 0), axis=0, keepdims=True
+    )
 
     lane = lax.broadcasted_iota(jnp.int32, (8, EXTENDED), 1)
     sub = lax.broadcasted_iota(jnp.int32, (8, EXTENDED), 0)
@@ -124,6 +135,18 @@
     def attend(g, carry):
         for c in kv_copies(g):
             c.wait()
+
+        @pl.when(g == 2)
+        def _():
+            for c in weights:
+                c.start()
+
+        for j in range(4):
+            first = g * 256 + j * 64
+            at = lax.broadcasted_iota(jnp.int32, (64, ROWS * 8), 0) + first
+            outward[pl.ds(pl.multiple_of(first, 64), 64), :] = jnp.where(
+                at == place_row[...], 1.0, 0.0
+            ).astype(jnp.bfloat16)
         rows = [g * GROUP + j for j in range(GROUP)]
         at = [pl.ds(pl.multiple_of(r * 8, 8), 8) for r in rows]
         scores = []
@@ -159,17 +182,17 @@
 
     lax.fori_loop(0, 4, fill, 0)
 
-    def dispatch(i, carry):
-        for j in range(7):
-            d = peer(i * 7 + j)
+    def dispatch(half):
+        def step(k, d):
             pltpu.make_async_remote_copy(
-                src_ref=send.at[d], dst_ref=recv.at[dp], send_sem=d_send, recv_sem=d_recv,
+                src_ref=send.at[d], dst_ref=recv.at[k], send_sem=d_send, recv_sem=d_recv.at[half],
                 device_id=(d, t), device_id_type=MESH,
             ).start()
-        return carry
-
-    lax.fori_loop(0, 9, dispatch, 0)
-    recv[dp] = send[dp]
+
+        each(4 * half, 4 * half + 4, ahead, 1, step)
+
+    dispatch(0)
+    recv[7] = send[dp]
 
     for h in range(2):
         for s in range(2):
@@ -205,73 +228,93 @@
         c = remote(i, bsend.at[i], brecv.at[i], near)
         c.start()
         base_near.append(c)
+    dispatch(1)
     for i in range(2):
 
         def to_keep(cols, value, i=i):
             keep[i, :, cols] = value
 
         base_block(2 + i, to_keep)
+
+    lane = lax.broadcasted_iota(jnp.int32, (ROWS, HEAD), 1)
+    for c in range(4):
+        for s in range(2):
+            for n in range(8):
+                homeward[(c * 2 + s) * ROWS : (c * 2 + s + 1) * ROWS, n * HEAD : (n + 1) * HEAD] = jnp.where(
+                    lane + (n * HEAD - s * 4 - c) == place_col[...], 1.0, 0.0
+                ).astype(jnp.bfloat16)
+
+    weights[4].wait()
+    weights[5].wait()
+
+    def give_back(k, d):
+        pltpu.make_async_remote_copy(
+            src_ref=rsend.at[k], dst_ref=rrecv.at[dp], send_sem=r_send, recv_sem=r_recv,
+            device_id=(d, t), device_id_type=MESH,
+        ).start()
+
+    others = (near, far, near_far)
+    mine = pl.ds(pl.multiple_of(t * 32, 32), 32)
+    for half in range(2):
+        blocks = slice(half * 32, half * 32 + 32)
+        count = 31 + half
+        arrived = recv.at[pl.ds(half * 32, count)]
+        pltpu.make_async_copy(arrived, arrived, d_recv.at[half]).wait()
+        for h in range(2):
+            recvf[h] = recv[blocks, :, h * HEAD : (h + 1) * HEAD].reshape(8 * ROWS, HEAD).astype(jnp.float32)
+        received = jnp.concatenate(
+            [
+                recvf[h, pl.ds(g, 2 * ROWS, stride=4), :].astype(jnp.bfloat16)
+                for h in range(2)
+                for g in range(4)
+            ],
+            1,
+        )
+        part[half] = jnp.dot(received, wd[...], preferred_element_type=jnp.float32)
+        sums = []
+        for i, other in enumerate(others):
+            rows = pl.ds(pl.multiple_of(other * 32, 32), 32)
+            c = remote(3 + half * 6 + i, part.at[half, rows], x1r.at[half, i], other)
+            c.start()
+            sums.append(c)
+        for c in sums:
+            c.wait()
+        total = part[half, mine, :] + x1r[half, 0] + (x1r[half, 1] + x1r[half, 2])
+        shrunk[half, mine, :] = total.astype(jnp.bfloat16)
+        shares = []
+        for i, other in enumerate(others):
+            c = remote(6 + half * 6 + i, shrunk.at[half, mine], shrunk.at[half, mine], other)
+            c.start()
+            shares.append(c)
+        for c in shares:
+            c.wait()
+        for c in range(4):
+            lifted = jnp.dot(shrunk[half], wu[:, c * 256 : (c + 1) * 256], preferred_element_type=jnp.float32)
+            for h in range(2):
+                liftf[h, pl.ds(c, 2 * ROWS, stride=4), :] = lifted[:, h * HEAD : (h + 1) * HEAD]
+        for h in range(2):
+            rsend[blocks, :, h * HEAD : (h + 1) * HEAD] = (
+                liftf[h].reshape(ROWS // 2, 16, HEAD).astype(jnp.bfloat16)
+            )
+        if half == 0:
+            rrecv[dp] = rsend[7]
+        each(4 * half, 4 * half + 4, behind, -1, give_back)
+
     base_near[1].wait()
     csend[...] = (keep[0] + brecv[1].astype(jnp.float32)).astype(jnp.bfloat16)
     base_far = remote(2, csend, crecv, far)
     base_far.start()
-
-    weights[4].wait()
-    weights[5].wait()
-    pltpu.make_async_copy(recv.at[pl.ds(0, 63)], recv.at[pl.ds(0, 63)], d_recv).wait()
-    for h in range(2):
-        recvf[h] = recv[:, :, h * HEAD : (h + 1) * HEAD].reshape(16 * ROWS, HEAD).astype(jnp.float32)
-    received = jnp.concatenate(
-        [recvf[h, pl.ds(g, 4 * ROWS, stride=4), :].astype(jnp.bfloat16) for h in range(2) for g in range(4)], 1
-    )
-    part[...] = jnp.dot(received, wd[...], preferred_element_type=jnp.float32)
-    mine = pl.ds(pl.multiple_of(core * 128, 128), 128)
-    theirs = pl.ds(pl.multiple_of((1 - core) * 128, 128), 128)
-    x1 = remote(3, part.at[theirs], x1r, near)
-    x1.start()
-    x1.wait()
-    pair_sum = part[mine, :] + x1r[...]
-    x2s[...] = pair_sum.astype(jnp.bfloat16)
-    x2 = remote(4, x2s, x2r, far)
-    x2.start()
-    x2.wait()
-    shrunk[mine, :] = (part[mine, :] + x1r[...] + x2r[...].astype(jnp.float32)).astype(jnp.bfloat16)
-    x3 = remote(5, shrunk.at[mine], shrunk.at[mine], near)
-    x3.start()
-    x3.wait()
-
-    for c in range(4):
-        lifted = jnp.dot(shrunk[...], wu[:, c * 256 : (c + 1) * 256], preferred_element_type=jnp.float32)
-        for h in range(2):
-            liftf[h, pl.ds(c, 4 * ROWS, stride=4), :] = lifted[:, h * HEAD : (h + 1) * HEAD]
-    for h in range(2):
-        rsend[:, :, h * HEAD : (h + 1) * HEAD] = liftf[h].reshape(ROWS, 16, HEAD).astype(jnp.bfloat16)
-    rrecv[dp] = rsend[dp]
-
-    def give_back(i, carry):
-        for j in range(7):
-            d = peer(i * 7 + j)
-            pltpu.make_async_remote_copy(
-                src_ref=rsend.at[d], dst_ref=rrecv.at[dp], send_sem=r_send, recv_sem=r_recv,
-                device_id=(d, t), device_id_type=MESH,
-            ).start()
-        return carry
-
-    lax.fori_loop(0, 9, give_back, 0)
-
     base_near[0].wait()
     base_far.wait()
     keep[1] = keep[1] + brecv[0].astype(jnp.float32) + crecv[...].astype(jnp.float32)
     pltpu.make_async_copy(rrecv.at[pl.ds(0, 63)], rrecv.at[pl.ds(0, 63)], r_recv).wait()
 
+    lifts = jnp.dot(homeward[...], rrecv[...].reshape(ROWS * 16, 256), preferred_element_type=jnp.float32)
     for c in range(4):
-        cols = slice(c * 256, (c + 1) * 256)
-        lifts = jnp.dot(
-            homeward[c * 128 : (c + 1) * 128, :], rrecv[...].reshape(ROWS * 16, 256), preferred_element_type=jnp.float32
-        )
         for s in range(2):
-            rows = slice(s * ROWS, (s + 1) * ROWS)
-            out_ref[s, :, cols] = (keep[1, rows, cols] + lifts[rows]).astype(jnp.bfloat16)
+            rows, first = slice(s * ROWS, (s + 1) * ROWS), (c * 2 + s) * ROWS
+            cols = slice(c * 256, (c + 1) * 256)
+            out_ref[s, :, cols] = (keep[1, rows, cols] + lifts[first : first + ROWS]).astype(jnp.bfloat16)
     pltpu.make_async_copy(send.at[pl.ds(0, 63)], send.at[pl.ds(0, 63)], d_send).wait()
     pltpu.make_async_copy(rsend.at[pl.ds(0, 63)], rsend.at[pl.ds(0, 63)], r_send).wait()
 
@@ -288,16 +331,6 @@
     opponent,
     cache_length_rows,
 ):
-    ids = opponent[:, 0]
-    place = jnp.arange(ROWS, dtype=jnp.int32)
-    earlier = (ids[:, None] == ids[None, :]) & (place[None, :] < place[:, None])
-    slot_of_row = 2 * ids + jnp.sum(earlier.astype(jnp.int32), axis=1)
-    eight = jnp.arange(8, dtype=jnp.int32)
-    place_row = (slot_of_row[:, None] * 8 + eight[None, :]).reshape(1, ROWS * 8)
-    quarter, step = jnp.arange(4, dtype=jnp.int32), jnp.arange(2, dtype=jnp.int32)
-    place_col = (
-        slot_of_row[None, None, :] * 8 + step[None, :, None] * 4 + quarter[:, None, None]
-    ).reshape(ROWS * 8, 1)
     bf16, f32 = jnp.bfloat16, jnp.float32
     vmem, dma = pltpu.VMEM, pltpu.SemaphoreType.DMA
     hbm = pl.BlockSpec(memory_space=pl.ANY)
@@ -305,7 +338,7 @@
     return pl.pallas_call(
         kernel,
         out_shape=jax.ShapeDtypeStruct((2, ROWS, 1024), bf16),
-        in_specs=[hbm] * 8 + [smem] + [pl.BlockSpec(memory_space=pltpu.VMEM)] * 2,
+        in_specs=[hbm] * 8 + [smem] + [pl.BlockSpec(memory_space=pltpu.VMEM)],
         out_specs=pl.BlockSpec(memory_space=pltpu.VMEM),
         scratch_shapes=[
             vmem((2, ROWS, 1024), bf16),
@@ -317,6 +350,8 @@
             vmem((2, ROWS * 8, HEAD), f32),
             vmem((2, ROWS * 8, HEAD), f32),
             vmem((ROWS * 8, 256), bf16),
+            vmem((1, ROWS * 8), jnp.int32),
+            vmem((ROWS, HEAD), jnp.int32),
             vmem((ROWS * 16, ROWS * 8), bf16),
             vmem((ROWS * 8, ROWS * 16), bf16),
             vmem((4, 1024, 1024), bf16),
@@ -324,13 +359,11 @@
             vmem((256, 1024), bf16),
             vmem((ROWS, 16, 256), bf16),
             vmem((ROWS, 16, 256), bf16),
-            vmem((2, ROWS * 16, HEAD), f32),
-            vmem((256, 256), f32),
-            vmem((128, 256), f32),
-            vmem((128, 256), bf16),
-            vmem((128, 256), bf16),
-            vmem((256, 256), bf16),
-            vmem((2, ROWS * 16, HEAD), f32),
+            vmem((2, ROWS * 8, HEAD), f32),
+            vmem((2, 128, 256), f32),
+            vmem((2, 3, 32, 256), f32),
+            vmem((2, 128, 256), bf16),
+            vmem((2, ROWS * 8, HEAD), f32),
             vmem((ROWS, 16, 256), bf16),
             vmem((ROWS, 16, 256), bf16),
             vmem((2 * ROWS, 1024), bf16),
@@ -343,11 +376,11 @@
             dma((2, 4)),
             dma((6,)),
             dma,
+            dma((2,)),
             dma,
             dma,
-            dma,
-            dma((6,)),
-            dma((6,)),
+            dma((15,)),
+            dma((15,)),
         ],
         compiler_params=pltpu.CompilerParams(
             collective_id=0, has_side_effects=True, vmem_limit_bytes=56 << 20
@@ -363,8 +396,7 @@
         adapter_down_weight,
         adapter_up_weight,
         cache_length_rows,
-        place_row,
-        place_col,
+        opponent.reshape(1, ROWS),
     )
 
 

time: 66.5 us -> 56.6 us (0.85)
  Pallas kernels: 60.7 us -> 54.9 us
  other arithmetic: 2.39 us -> 0 us
  local copies, waits for them, and re-layouts: 3.25 us -> 1.67 us
    pallas_call x1, Pallas kernels: 60.7 us -> 54.9 us  [local(): pl.pallas_call(kernel, out_shape=jax.ShapeDtypeStruct((2, ROWS, 1024), bf...]
    add x2 -> x0, local copies, waits for them, and re-layouts: 1.58 us -> none  [the longest x1 0.91 us: local(): slot_of_row[None, None, :] * 8 + step[None, :, None] * 4]
    reduce_sum x1 -> x0, other arithmetic: 0.91 us -> none  [local(): slot_of_row = 2 * ids + jnp.sum(earlier.astype(jnp.int32), axis=1)]
    add x4 -> x0, other arithmetic: 0.81 us -> none  [the longest x2 0.73 us: local(): place_row = (slot_of_row[:, None] * 8 + eight[None, :]).reshape(1, ROWS * 8)]
    mul x2 -> x0, other arithmetic: 0.67 us -> none  [the longest x1 0.67 us: local(): slot_of_row[None, None, :] * 8 + step[None, :, None] * 4]
where the time goes in v2:
time: 56.6 us; the launch traced here: 56.5 us
  Pallas kernels  54.9 us (97%)
  local copies, waits for them, and re-layouts  1.67 us (3%)
    pallas_call x1, Pallas kernels, local(): pl.pallas_call(kernel, out_shape=jax.ShapeDtypeStruct((2, ROWS, 1024), bf...  54.9 us
    unnamed x1, local copies, waits for them, and re-layouts  1.67 us

profile of v2, /device:TPU:1, one launch (start us, length us, event | category | flops | bytes accessed | tf_op | source)
XLA Modules:
  0.0 56.5 jit_solution(15238500964818948247)
XLA Ops:
  0.0 54.9 %shard_map.100 = bf16[2,64,1024]{2,1,0:T(8,128)(2,1)} custom-call(bf16[2,64,1024]{2,1,0:T(8,128)(2,1)} %q_hbm.1, bf16[64,192,256]{2,1,0:T(8,128)(2,1)} %k_hbm.1, bf16[64,192,256]{2,1,0:T(8,128)(2,1)} %v_hbm.1, bf16[2,64,256]{2,1,0:T(8,128)(2,1)} %nk_hbm.1, bf16[2,64,256]{2,1,0:T(8,128)(2,1)} %nv_hbm.1, bf16[1024,4096]{1,0:T(8,128)(2,1)} %wo_hbm.1, ...), custom_call_target="tpu_custom_call" | custom-call | flops 1500000000 | bytes 24000000 | tf_op jit(solution)/shard_map/pallas_call | solution.py:338
  54.9 1.7 %copy.12 = bf16[2,64,1024]{2,1,0:T(8,128)(2,1)} copy(bf16[2,64,1024]{2,1,0:T(8,128)(2,1)} %shard_map.100) | data formatting | bytes 524288

commit v3 on v2

--- a/solution.py
+++ b/solution.py
@@ -21,7 +21,7 @@
     q_hbm, k_hbm, v_hbm, nk_hbm, nv_hbm, wo_hbm, wd_hbm, wu_hbm, len_ref, opp_ref,
     out_ref,
     qv, nkv, nvv, kb, vb, fresh, qs, att, attp, place_row, place_col, outward, homeward, wo, wd, wu,
-    send, recv, recvf, part, x1r, shrunk, liftf, rsend, rrecv,
+    send, recv, recvf, part, x1r, pair, x2r, shrunk, liftf, rsend, rrecv,
     attb, bsend, brecv, keep, csend, crecv,
     small_sem, kv_sem, w_sem, d_send, d_recv, r_send, r_recv, t_send, t_recv,
 ):
@@ -218,23 +218,32 @@
             device_id=(dp, other), device_id_type=MESH,
         )
 
-    base_near = []
-    for i in range(2):
-
-        def to_send(cols, value, i=i):
+    def send_near(i):
+        def to_send(cols, value):
             bsend[i, :, cols] = value.astype(jnp.bfloat16)
 
         base_block(i, to_send)
         c = remote(i, bsend.at[i], brecv.at[i], near)
         c.start()
-        base_near.append(c)
+        return c
+
+    def keep_block(i):
+        def to_keep(cols, value):
+            keep[i, :, cols] = value
+
+        base_block(2 + i, to_keep)
+
+    for_far = send_near(1)
+    keep_block(0)
+    for_far.wait()
+    csend[...] = (keep[0] + brecv[1].astype(jnp.float32)).astype(jnp.bfloat16)
+    base_far = [
+        remote(2 + i, csend.at[pl.ds(i * ROWS, ROWS)], crecv.at[pl.ds(i * ROWS, ROWS)], far) for i in range(2)
+    ]
+    base_far[0].start()
     dispatch(1)
-    for i in range(2):
-
-        def to_keep(cols, value, i=i):
-            keep[i, :, cols] = value
-
-        base_block(2 + i, to_keep)
+    base_near = send_near(0)
+    keep_block(1)
 
     lane = lax.broadcasted_iota(jnp.int32, (ROWS, HEAD), 1)
     for c in range(4):
@@ -253,8 +262,6 @@
             device_id=(d, t), device_id_type=MESH,
         ).start()
 
-    others = (near, far, near_far)
-    mine = pl.ds(pl.multiple_of(t * 32, 32), 32)
     for half in range(2):
         blocks = slice(half * 32, half * 32 + 32)
         count = 31 + half
@@ -271,23 +278,16 @@
             1,
         )
         part[half] = jnp.dot(received, wd[...], preferred_element_type=jnp.float32)
-        sums = []
-        for i, other in enumerate(others):
-            rows = pl.ds(pl.multiple_of(other * 32, 32), 32)
-            c = remote(3 + half * 6 + i, part.at[half, rows], x1r.at[half, i], other)
-            c.start()
-            sums.append(c)
-        for c in sums:
-            c.wait()
-        total = part[half, mine, :] + x1r[half, 0] + (x1r[half, 1] + x1r[half, 2])
-        shrunk[half, mine, :] = total.astype(jnp.bfloat16)
-        shares = []
-        for i, other in enumerate(others):
-            c = remote(6 + half * 6 + i, shrunk.at[half, mine], shrunk.at[half, mine], other)
-            c.start()
-            shares.append(c)
-        for c in shares:
-            c.wait()
+        c = remote(4 + half * 2, part.at[half], x1r.at[half], near)
+        c.start()
+        c.wait()
+        pair[half] = (part[half] + x1r[half]).astype(jnp.bfloat16)
+        c = remote(5 + half * 2, pair.at[half], x2r.at[half], far)
+        c.start()
+        c.wait()
+        if half == 1:
+            base_far[1].start()
+        shrunk[half] = (part[half] + x1r[half] + x2r[half].astype(jnp.float32)).astype(jnp.bfloat16)
         for c in range(4):
             lifted = jnp.dot(shrunk[half], wu[:, c * 256 : (c + 1) * 256], preferred_element_type=jnp.float32)
             for h in range(2):
@@ -300,12 +300,9 @@
             rrecv[dp] = rsend[7]
         each(4 * half, 4 * half + 4, behind, -1, give_back)
 
-    base_near[1].wait()
-    csend[...] = (keep[0] + brecv[1].astype(jnp.float32)).astype(jnp.bfloat16)
-    base_far = remote(2, csend, crecv, far)
-    base_far.start()
-    base_near[0].wait()
-    base_far.wait()
+    base_near.wait()
+    for c in base_far:
+        c.wait()
     keep[1] = keep[1] + brecv[0].astype(jnp.float32) + crecv[...].astype(jnp.float32)
     pltpu.make_async_copy(rrecv.at[pl.ds(0, 63)], rrecv.at[pl.ds(0, 63)], r_recv).wait()
 
@@ -361,7 +358,9 @@
             vmem((ROWS, 16, 256), bf16),
             vmem((2, ROWS * 8, HEAD), f32),
             vmem((2, 128, 256), f32),
-            vmem((2, 3, 32, 256), f32),
+            vmem((2, 128, 256), f32),
+            vmem((2, 128, 256), bf16),
+            vmem((2, 128, 256), bf16),
             vmem((2, 128, 256), bf16),
             vmem((2, ROWS * 8, HEAD), f32),
             vmem((ROWS, 16, 256), bf16),
@@ -379,8 +378,8 @@
             dma((2,)),
             dma,
             dma,
-            dma((15,)),
-            dma((15,)),
+            dma((8,)),
+            dma((8,)),
         ],
         compiler_params=pltpu.CompilerParams(
             collective_id=0, has_side_effects=True, vmem_limit_bytes=56 << 20

time: 56.6 us -> 52.2 us (0.922)
  Pallas kernels: 54.9 us -> 50.4 us
    pallas_call x1, Pallas kernels: 54.9 us -> 50.4 us  [local(): pl.pallas_call(kernel, out_shape=jax.ShapeDtypeStruct((2, ROWS, 1024), bf...]
where the time goes in v3:
time: 52.2 us; the launch traced here: 52.1 us
  Pallas kernels  50.4 us (97%)
  local copies, waits for them, and re-layouts  1.67 us (3%)
    pallas_call x1, Pallas kernels, local(): pl.pallas_call(kernel, out_shape=jax.ShapeDtypeStruct((2, ROWS, 1024), bf...  50.4 us
    unnamed x1, local copies, waits for them, and re-layouts  1.67 us

profile of v3, /device:TPU:1, one launch (start us, length us, event | category | flops | bytes accessed | tf_op | source)
XLA Modules:
  0.0 52.1 jit_solution(6398534163439331611)
XLA Ops:
  0.0 50.4 %shard_map.100 = bf16[2,64,1024]{2,1,0:T(8,128)(2,1)} custom-call(bf16[2,64,1024]{2,1,0:T(8,128)(2,1)} %q_hbm.1, bf16[64,192,256]{2,1,0:T(8,128)(2,1)} %k_hbm.1, bf16[64,192,256]{2,1,0:T(8,128)(2,1)} %v_hbm.1, bf16[2,64,256]{2,1,0:T(8,128)(2,1)} %nk_hbm.1, bf16[2,64,256]{2,1,0:T(8,128)(2,1)} %nv_hbm.1, bf16[1024,4096]{1,0:T(8,128)(2,1)} %wo_hbm.1, ...), custom_call_target="tpu_custom_call" | custom-call | flops 1500000000 | bytes 24000000 | tf_op jit(solution)/shard_map/pallas_call | solution.py:335
  50.5 1.7 %copy.12 = bf16[2,64,1024]{2,1,0:T(8,128)(2,1)} copy(bf16[2,64,1024]{2,1,0:T(8,128)(2,1)} %shard_map.100) | data formatting | bytes 524288

commit v4 on v3

--- a/solution.py
+++ b/solution.py
@@ -136,7 +136,7 @@
         for c in kv_copies(g):
             c.wait()
 
-        @pl.when(g == 2)
+        @pl.when(g == 3)
         def _():
             for c in weights:
                 c.start()

time: 52.2 us -> 52.2 us (level)
  no operation moved by 1% of the time
where the time goes in v4:
time: 52.2 us; the launch traced here: 52.1 us
  Pallas kernels  50.4 us (97%)
  local copies, waits for them, and re-layouts  1.67 us (3%)
    pallas_call x1, Pallas kernels, local(): pl.pallas_call(kernel, out_shape=jax.ShapeDtypeStruct((2, ROWS, 1024), bf...  50.4 us
    unnamed x1, local copies, waits for them, and re-layouts  1.67 us

profile of v4, /device:TPU:1, one launch (start us, length us, event | category | flops | bytes accessed | tf_op | source)
XLA Modules:
  0.0 52.1 jit_solution(12903025807134518085)
XLA Ops:
  0.0 50.4 %shard_map.100 = bf16[2,64,1024]{2,1,0:T(8,128)(2,1)} custom-call(bf16[2,64,1024]{2,1,0:T(8,128)(2,1)} %q_hbm.1, bf16[64,192,256]{2,1,0:T(8,128)(2,1)} %k_hbm.1, bf16[64,192,256]{2,1,0:T(8,128)(2,1)} %v_hbm.1, bf16[2,64,256]{2,1,0:T(8,128)(2,1)} %nk_hbm.1, bf16[2,64,256]{2,1,0:T(8,128)(2,1)} %nv_hbm.1, bf16[1024,4096]{1,0:T(8,128)(2,1)} %wo_hbm.1, ...), custom_call_target="tpu_custom_call" | custom-call | flops 1500000000 | bytes 24000000 | tf_op jit(solution)/shard_map/pallas_call | solution.py:335
  50.4 1.7 %copy.12 = bf16[2,64,1024]{2,1,0:T(8,128)(2,1)} copy(bf16[2,64,1024]{2,1,0:T(8,128)(2,1)} %shard_map.100) | data formatting | bytes 524288
